TPU v7x, 32 devices: a whole 2x2x4 slice. The times are simulated.
32 devices in a mesh: sec: 2 (over y), row: 4 (over x, core), col: 4 (over z).
Axes of the slice: x: 2, y: 2, z: 4, core: 2. Of those that a mesh axis runs over, the one named last changes fastest.
Arguments:
- sketch: float32 [32, 64, 2048], P(None, ('sec', 'row'), 'col'), parts along dimension 1, may hold values from -6 to 6
- weights: float32 [8, 64, 2048], P(None, ('sec', 'row'), 'col'), parts along dimension 1, may hold values from 0.05 to 1
Outputs:
- basis: float32 [32, 64, 2048], P(None, ('sec', 'row'), 'col'), parts along dimension 1
- factor: float32 [64, 32], P('sec'), parts along dimension 0
There are 2 independent parts, one for each index of `sec`. A program takes and returns all parts, laid end to end along the dimension named above; each array names one. Nothing has to cross between parts.
All inputs are finite; a program needn't handle non-finite values.
Results may differ from a plain program's by a relative error of at most 0.0001.
Values sent between devices are 32-bit elements; how exact they have to be, the bound alone decides.
A program may use at most 64 MiB of HBM per device.

v0:
```python
import jax
import jax.numpy as jnp
from jax import lax
from jax.sharding import PartitionSpec as P

ITERS = 2


NEIGHBOURS = ((-1, -1), (-1, 0), (-1, 1), (0, -1), (0, 1), (1, -1), (1, 0), (1, 1))


def padded_2(block, sides, width):
    for axis, dim in sides:
        count = lax.axis_size(axis)
        forward = [(i, i + 1) for i in range(count - 1)]
        backward = [(target, source) for source, target in forward]
        low = lax.ppermute(
            lax.slice_in_dim(block, block.shape[dim] - width, None, axis=dim), axis, forward
        )
        high = lax.ppermute(lax.slice_in_dim(block, 0, width, axis=dim), axis, backward)
        block = jnp.concatenate([low, block, high], axis=dim)
    return block


def stencil(padded, local_weights):
    height = local_weights.shape[1]
    breadth = local_weights.shape[2]
    centre = padded[:, 1 : 1 + height, 1 : 1 + breadth]
    summed = jnp.sum(local_weights, axis=0) * centre
    for position, offset in enumerate(NEIGHBOURS):
        shift_row = offset[0]
        shift_col = offset[1]
        summed = (
            summed
            + local_weights[position]
            * padded[
                :, 1 + shift_row : 1 + shift_row + height, 1 + shift_col : 1 + shift_col + breadth
            ]
        )
    return summed


def factorize(interior, pixel_count):
    columns = interior.shape[0]
    flattened = interior.reshape(columns, -1)
    gram_local = jnp.dot(flattened, flattened.T, precision=lax.Precision.HIGHEST) / pixel_count
    summed = lax.psum(gram_local, ("row", "col"))
    return jnp.linalg.cholesky(summed)


def solve_planes(lower_tri, image_vals):
    columns = image_vals.shape[0]
    solved = jax.scipy.linalg.solve_triangular(
        lower_tri, image_vals.reshape(columns, -1), lower=True
    )
    return solved.reshape(image_vals.shape)


def on_device(sketch, weights):
    tile_rows = sketch.shape[1]
    tile_cols = sketch.shape[2]
    pixel_count = tile_rows * tile_cols * lax.axis_size("row") * lax.axis_size("col")
    wide_weights = padded_2(weights, (("row", 1), ("col", 2)), ITERS - 1)
    sketch_field = padded_2(sketch, (("row", 1), ("col", 2)), ITERS)
    for power_step in range(ITERS):
        margin = ITERS - 1 - power_step
        local_weights = wide_weights[
            :,
            power_step : power_step + tile_rows + 2 * margin,
            power_step : power_step + tile_cols + 2 * margin,
        ]
        image_vals = stencil(sketch_field, local_weights)
        interior = image_vals[:, margin : margin + tile_rows, margin : margin + tile_cols]
        lower_tri = factorize(interior, pixel_count)
        sketch_field = solve_planes(lower_tri, image_vals)
    return (sketch_field, lower_tri.T)


def solution(mesh):
    return jax.shard_map(
        on_device,
        mesh=mesh,
        in_specs=(P(None, ("sec", "row"), "col"), P(None, ("sec", "row"), "col")),
        out_specs=(P(None, ("sec", "row"), "col"), P("sec", None)),
        check_vma=False,
    )
```

profile of v0, /device:TPU:0, one launch (start us, length us, event | category | flops | bytes accessed | tf_op | source)
XLA Modules:
  0.0 178.7 jit_solution(1603129696953447877)
XLA Ops:
  0.6 1.1 fusion.45
  1.7 2.4 %collective-permute-start = (f32[8,1,512]{2,1,0:T(1,128)S(1)}, f32[8,1,512]{2,1,0:T(1,128)S(1)}, u32[]{:S(2)}, u32[]{:S(2)}) collective-permute-start(f32[8,1,512]{2,1,0:T(1,128)S(1)} %get-tuple-element.31), channel_id=1, source_target_pairs={{0,4},{4,8},{8,12},{1,5},{5,9},{9,13},{2,6},{6,10},{10,14},{3,7},{... | collective-permute-start | bytes 49160 | tf_op jit(solution)/shard_map/ppermute | solution.py:17
  4.1 1.4 collective-permute-start.1
  5.5 1.4 fusion.44
  6.9 5.1 %collective-permute-start.4 = (f32[32,2,512]{2,0,1:T(8,128)S(1)}, f32[32,2,512]{2,0,1:T(8,128)S(1)}, u32[]{:S(2)}, u32[]{:S(2)}) collective-permute-start(f32[32,2,512]{2,0,1:T(8,128)S(1)} %copy.47), channel_id=1, source_target_pairs={{0,4},{4,8},{8,12},{1,5},{5,9},{9,13},{2,6},{6,10},{10,14},{3,7},{... | collective-permute-start | bytes 393224 | tf_op jit(solution)/shard_map/ppermute | solution.py:17
  12.1 1.3 collective-permute-start.5
  13.4 0.9 pad_maximum_fusion.6
  14.3 3.5 %collective-permute-start.2 = (f32[8,10,1]{2,1,0:T(8,128)S(1)}, f32[8,10,1]{2,1,0:T(8,128)S(1)}, u32[]{:S(2)}, u32[]{:S(2)}) collective-permute-start(f32[8,10,1]{2,1,0:T(8,128)S(1)} %get-tuple-element.21), channel_id=1, source_target_pairs={{0,1},{1,2},{2,3},{4,5},{5,6},{6,7},{8,9},{9,10},{10,11},{12,13},{... | collective-permute-start | bytes 968 | tf_op jit(solution)/shard_map/ppermute | solution.py:17
  17.8 1.3 collective-permute-start.3
  19.2 0.5 collective-permute-done.2
  19.7 4.3 %collective-permute-done.3 = f32[8,10,1]{2,1,0:T(8,128)S(1)} collective-permute-done((f32[8,10,1]{2,1,0:T(8,128)S(1)}, f32[8,10,1]{2,1,0:T(8,128)S(1)}, u32[]{:S(2)}, u32[]{:S(2)}) %collective-permute-start.3) | collective-permute-done | bytes 352 | tf_op jit(solution)/shard_map/ppermute | solution.py:20
  24.8 3.5 %collective-permute-start.6 = (f32[32,12,2]{2,0,1:T(8,128)S(1)}, f32[32,12,2]{2,0,1:T(8,128)S(1)}, u32[]{:S(2)}, u32[]{:S(2)}) collective-permute-start(f32[32,12,2]{2,0,1:T(8,128)S(1)} %get-tuple-element.7), channel_id=1, source_target_pairs={{0,1},{1,2},{2,3},{4,5},{5,6},{6,7},{8,9},{9,10},{10,11},{12,13},{... | collective-permute-start | bytes 9224 | tf_op jit(solution)/shard_map/ppermute | solution.py:17
  28.3 1.3 collective-permute-start.7
  29.6 3.9 %collective-permute-done.6 = f32[32,12,2]{2,0,1:T(8,128)S(1)} collective-permute-done((f32[32,12,2]{2,0,1:T(8,128)S(1)}, f32[32,12,2]{2,0,1:T(8,128)S(1)}, u32[]{:S(2)}, u32[]{:S(2)}) %collective-permute-start.6) | collective-permute-done | bytes 3104 | tf_op jit(solution)/shard_map/ppermute | solution.py:17
  33.5 4.1 %collective-permute-done.7 = f32[32,12,2]{2,0,1:T(8,128)S(1)} collective-permute-done((f32[32,12,2]{2,0,1:T(8,128)S(1)}, f32[32,12,2]{2,0,1:T(8,128)S(1)}, u32[]{:S(2)}, u32[]{:S(2)}) %collective-permute-start.7) | collective-permute-done | bytes 3104 | tf_op jit(solution)/shard_map/ppermute | solution.py:20
  38.0 1.4 fusion.7
  39.4 0.7 fusion.1
  40.6 59.4 %psum.14 = f32[32,32]{0,1:T(8,128)S(1)} all-reduce(f32[32,32]{0,1:T(8,128)S(1)} %fusion.1), channel_id=1, replica_groups=mesh['sec'=2,'row'=4,'col'=4] {'row','col'}, use_global_device_ids=true, to_apply=%region_2.3 | all-reduce | flops 1024 | bytes 8192 | tf_op jit(solution)/shard_map/psum | solution.py:47
  100.1 2.9 %cholesky.44 = f32[32,32]{1,0:T(8,128)S(1)} custom-call(f32[32,32]{1,0:T(8,128)S(1)} %fusion.38), custom_call_target="Cholesky" | custom-call | tf_op jit(solution)/shard_map/jit(cholesky)/cholesky | solution.py:48
  103.1 0.6 compare_reduce_fusion.1
  103.7 0.7 fusion.34
  104.4 2.4 %custom-call.10 = f32[1,32,32]{1,2,0:T(8,128)S(1)} custom-call(f32[1,32,32]{2,1,0:T(8,128)S(1)} %fusion.34), custom_call_target="InvertDiagBlocksLowerTriangular" | custom-call | tf_op jit(solution)/shard_map/jit(_solve_triangular)/triangular_solve | solution.py:53
  107.7 1.0 fusion.20
  108.7 2.1 %fusion = f32[32,32]{0,1:T(8,128)S(1)} fusion(f32[32,10,514]{2,0,1:T(8,128)S(1)} %fusion.20, f32[8,512]{1,0:T(8,128)S(1)} %get-tuple-element.29, f32[8,512]{1,0:T(8,128)S(1)} %get-tuple-element.30, f32[8,512]{1,0:T(8,128)S(1)} %get-tuple-element.24, f32[8,512]{1,0:T(8,128)S(1)} %get-tuple-element.25, f32[8,512]{1,0:T(8,128)S(1)} %get-tuple-element.26, ...), kind=kOutput, calls=%fused_computation.5 | convolution fusion | flops 54789120 | bytes 9736192 | tf_op jit(solution)/shard_map/dot_general | solution.py:46
  110.8 58.0 %psum.15 = f32[32,32]{0,1:T(8,128)S(1)} all-reduce(f32[32,32]{0,1:T(8,128)S(1)} %fusion), channel_id=1, replica_groups=mesh['sec'=2,'row'=4,'col'=4] {'row','col'}, use_global_device_ids=true, to_apply=%region_5.7 | all-reduce | flops 1024 | bytes 8192 | tf_op jit(solution)/shard_map/psum | solution.py:47
  168.8 2.9 %cholesky.55 = f32[32,32]{1,0:T(8,128)S(1)} custom-call(f32[32,32]{1,0:T(8,128)S(1)} %fusion.37), custom_call_target="Cholesky" | custom-call | tf_op jit(solution)/shard_map/jit(cholesky)/cholesky | solution.py:48
  171.7 0.6 compare_reduce_fusion
  172.4 0.7 fusion.41
  173.0 2.4 %custom-call.11 = f32[1,32,32]{1,2,0:T(8,128)S(1)} custom-call(f32[1,32,32]{2,1,0:T(8,128)S(1)} %get-tuple-element.34), custom_call_target="InvertDiagBlocksLowerTriangular" | custom-call | tf_op jit(solution)/shard_map/jit(_solve_triangular)/triangular_solve | solution.py:53
  175.5 1.4 fusion.22
  176.9 1.1 copy.28
  178.0 0.7 copy.29
  (28 shorter events, 2.8 us)
Async XLA Ops:
  0.6 18.5 %copy-start = (f32[8,8,512]{2,1,0:T(8,128)S(1)}, f32[8,8,512]{2,1,0:T(8,128)}, u32[]{:S(2)}) copy-start(f32[8,8,512]{2,1,0:T(8,128)} %param.4) | copy-start | bytes 393220
  1.7 11.7 %collective-permute-start = (f32[8,1,512]{2,1,0:T(1,128)S(1)}, f32[8,1,512]{2,1,0:T(1,128)S(1)}, u32[]{:S(2)}, u32[]{:S(2)}) collective-permute-start(f32[8,1,512]{2,1,0:T(1,128)S(1)} %get-tuple-element.31), channel_id=1, source_target_pairs={{0,4},{4,8},{8,12},{1,5},{5,9},{9,13},{2,6},{6,10},{10,14},{3,7},{... | collective-permute-start | bytes 49160 | tf_op jit(solution)/shard_map/ppermute | solution.py:17
  4.1 20.2 %copy-start.1 = (f32[32,8,512]{2,1,0:T(8,128)S(1)}, f32[32,8,512]{2,1,0:T(8,128)}, u32[]{:S(2)}) copy-start(f32[32,8,512]{2,1,0:T(8,128)} %param.3) | copy-start | bytes 1572868
  4.1 9.3 %collective-permute-start.1 = (f32[8,1,512]{2,1,0:T(1,128)S(1)}, f32[8,1,512]{2,1,0:T(1,128)S(1)}, u32[]{:S(2)}, u32[]{:S(2)}) collective-permute-start(f32[8,1,512]{2,1,0:T(1,128)S(1)} %get-tuple-element.32), channel_id=1, source_target_pairs={{4,0},{8,4},{12,8},{5,1},{9,5},{13,9},{6,2},{10,6},{14,10},{7,3},{... | collective-permute-start | bytes 49160 | tf_op jit(solution)/shard_map/ppermute | solution.py:20
  6.9 17.3 %collective-permute-start.4 = (f32[32,2,512]{2,0,1:T(8,128)S(1)}, f32[32,2,512]{2,0,1:T(8,128)S(1)}, u32[]{:S(2)}, u32[]{:S(2)}) collective-permute-start(f32[32,2,512]{2,0,1:T(8,128)S(1)} %copy.47), channel_id=1, source_target_pairs={{0,4},{4,8},{8,12},{1,5},{5,9},{9,13},{2,6},{6,10},{10,14},{3,7},{... | collective-permute-start | bytes 393224 | tf_op jit(solution)/shard_map/ppermute | solution.py:17
  12.1 12.5 %collective-permute-start.5 = (f32[32,2,512]{2,0,1:T(8,128)S(1)}, f32[32,2,512]{2,0,1:T(8,128)S(1)}, u32[]{:S(2)}, u32[]{:S(2)}) collective-permute-start(f32[32,2,512]{2,0,1:T(8,128)S(1)} %copy.48), channel_id=1, source_target_pairs={{4,0},{8,4},{12,8},{5,1},{9,5},{13,9},{6,2},{10,6},{14,10},{7,3},{... | collective-permute-start | bytes 393224 | tf_op jit(solution)/shard_map/ppermute | solution.py:20
  14.3 5.4 %collective-permute-start.2 = (f32[8,10,1]{2,1,0:T(8,128)S(1)}, f32[8,10,1]{2,1,0:T(8,128)S(1)}, u32[]{:S(2)}, u32[]{:S(2)}) collective-permute-start(f32[8,10,1]{2,1,0:T(8,128)S(1)} %get-tuple-element.21), channel_id=1, source_target_pairs={{0,1},{1,2},{2,3},{4,5},{5,6},{6,7},{8,9},{9,10},{10,11},{12,13},{... | collective-permute-start | bytes 968 | tf_op jit(solution)/shard_map/ppermute | solution.py:17
  17.8 6.2 %collective-permute-start.3 = (f32[8,10,1]{2,1,0:T(8,128)S(1)}, f32[8,10,1]{2,1,0:T(8,128)S(1)}, u32[]{:S(2)}, u32[]{:S(2)}) collective-permute-start(f32[8,10,1]{2,1,0:T(8,128)S(1)} %get-tuple-element.22), channel_id=1, source_target_pairs={{1,0},{2,1},{3,2},{5,4},{6,5},{7,6},{9,8},{10,9},{11,10},{13,12},{... | collective-permute-start | bytes 968 | tf_op jit(solution)/shard_map/ppermute | solution.py:20
  24.8 8.8 %collective-permute-start.6 = (f32[32,12,2]{2,0,1:T(8,128)S(1)}, f32[32,12,2]{2,0,1:T(8,128)S(1)}, u32[]{:S(2)}, u32[]{:S(2)}) collective-permute-start(f32[32,12,2]{2,0,1:T(8,128)S(1)} %get-tuple-element.7), channel_id=1, source_target_pairs={{0,1},{1,2},{2,3},{4,5},{5,6},{6,7},{8,9},{9,10},{10,11},{12,13},{... | collective-permute-start | bytes 9224 | tf_op jit(solution)/shard_map/ppermute | solution.py:17
  28.3 9.3 %collective-permute-start.7 = (f32[32,12,2]{2,0,1:T(8,128)S(1)}, f32[32,12,2]{2,0,1:T(8,128)S(1)}, u32[]{:S(2)}, u32[]{:S(2)}) collective-permute-start(f32[32,12,2]{2,0,1:T(8,128)S(1)} %get-tuple-element.8), channel_id=1, source_target_pairs={{1,0},{2,1},{3,2},{5,4},{6,5},{7,6},{9,8},{10,9},{11,10},{13,12},{... | collective-permute-start | bytes 9224 | tf_op jit(solution)/shard_map/ppermute | solution.py:20
where the time goes:
time: 179 us
  blocking collectives  117 us (65%)
  starting transfers between devices  19.8 us (11%)
  other arithmetic  16.3 us (9%)
  waiting for transfers between devices  12.8 us (7%)
  local copies, waits for them, and re-layouts  6.29 us (4%)
  matrix products  5.25 us (3%)
    psum x2, blocking collectives, factorize(): summed = lax.psum(gram_local, ('row', 'col'))  117 us
    ppermute x4, starting transfers between devices, padded_2(): lax.ppermute(lax.slice_in_dim(block, block.shape[dim] - width, None, axis...  14.5 us
    ppermute x4, waiting for transfers between devices, padded_2(): lax.ppermute(lax.slice_in_dim(block, 0, width, axis=dim), axis, backward)  8.38 us
    another operation x6, other arithmetic, factorize(): return jnp.linalg.cholesky(summed)  7.19 us
    another operation x3, other arithmetic, solve_planes(): jax.scipy.linalg.solve_triangular(lower_tri, image_vals.reshape(columns,...  5.52 us
    ppermute x4, starting transfers between devices, padded_2(): lax.ppermute(lax.slice_in_dim(block, 0, width, axis=dim), axis, backward)  5.3 us
    ppermute x4, waiting for transfers between devices, padded_2(): lax.ppermute(lax.slice_in_dim(block, block.shape[dim] - width, None, axis...  4.46 us
  transfers between devices with their start and end apart: 8, of which 4 were waited for; matrix products, arithmetic and copies ran while one was open for 2% of the time, Pallas kernels for 0%

commit v1 on v0

v1 whole, which is shorter than its diff:
```python
import functools

import jax
import jax.numpy as jnp
from jax import lax
from jax.experimental import pallas as pl
from jax.experimental.pallas import tpu as pltpu
from jax.sharding import PartitionSpec as P

LANES = 128
SUB = 8
NEIGHBOURS = ((-1, -1), (-1, 0), (-1, 1), (0, -1), (0, 1), (1, -1), (1, 0), (1, 1))
MESH = pl.DeviceIdType.MESH
NT = (((1,), (1,)), ((), ()))
HIGHEST = lax.Precision.HIGHEST


def split(x):
    hi = x.astype(jnp.bfloat16)
    lo = (x - hi.astype(jnp.float32)).astype(jnp.bfloat16)
    return hi, lo


def kernel(
    n, rows, cols, R, C,
    sk_hbm, w_hbm, out_ref, fac_ref,
    raw, wraw, staged, ext, y1, y2, pack, nb, gr, gc, gsend1, gsend2,
    load_sem, store_sem, row_send, row_recv, nb_send, nb_recv, gr_send, gr_recv, gc_send, gc_recv,
):
    groups = n // SUB
    all_groups = groups + 1
    wide = cols + LANES
    i = lax.axis_index("row")
    j = lax.axis_index("col")
    has_up, has_down = i > 0, i < R - 1
    has_left, has_right = j > 0, j < C - 1

    tiles = cols // LANES
    loads = []
    for t in range(tiles):
        across = pl.ds(t * LANES, LANES)
        loads.append(pltpu.make_async_copy(sk_hbm.at[:, across], raw.at[t], load_sem.at[0, t]))
        loads.append(pltpu.make_async_copy(w_hbm.at[:, across], wraw.at[t], load_sem.at[1, t]))
    for load in loads:
        load.start()

    barrier = pltpu.get_barrier_semaphore()
    for d in range(1, R):
        pl.semaphore_signal(
            barrier, inc=1, device_id={"row": lax.rem(i + d, R), "col": j}, device_id_type=MESH
        )
    for d in range(1, C):
        pl.semaphore_signal(
            barrier, inc=1, device_id={"row": i, "col": lax.rem(j + d, C)}, device_id_type=MESH
        )
    ups = ((-1, has_up), (0, None), (1, has_down))
    sides = ((-1, has_left), (1, has_right))
    for dr, ok_r in ups:
        for dc, ok_c in sides:
            if dr != 0:
                @pl.when(jnp.logical_and(ok_r, ok_c))
                def _(dr=dr, dc=dc):
                    pl.semaphore_signal(
                        barrier, inc=1, device_id={"row": i + dr, "col": j + dc},
                        device_id_type=MESH,
                    )
    diagonals = (has_up.astype(jnp.int32) + has_down.astype(jnp.int32)) * (
        has_left.astype(jnp.int32) + has_right.astype(jnp.int32)
    )

    lane = lax.broadcasted_iota(jnp.int32, (SUB, LANES), 1)

    def relayout(r):
        for t in range(tiles):
            across = slice(t * LANES, (t + 1) * LANES)
            for g in range(groups):
                ext[r + 2, g * SUB : (g + 1) * SUB, across] = raw[
                    t, pl.ds(g * SUB * rows + r, SUB, stride=rows), :
                ]
            ext[r + 2, n : n + SUB, across] = wraw[t, pl.ds(r, SUB, stride=rows), :]

    for load in loads:
        load.wait()
    for r in range(rows):
        relayout(r)

    packed = [jnp.zeros((SUB, LANES), jnp.float32), jnp.zeros((SUB, LANES), jnp.float32)]
    for r in range(rows):
        for g in range(all_groups):
            which, slot = (0, r * groups + g) if g < groups else (1, r)
            edge = jnp.where(
                lane < LANES // 2,
                ext[r + 2, g * SUB : (g + 1) * SUB, 0:LANES],
                ext[r + 2, g * SUB : (g + 1) * SUB, cols - LANES : cols],
            )
            moved = pltpu.roll(edge, (4 * slot + 2) % LANES, 1)
            packed[which] = jnp.where(lane // 4 == slot, moved, packed[which])
    pack[0:SUB, :] = packed[0]
    pack[SUB : 2 * SUB, :] = packed[1]

    pl.semaphore_wait(barrier, (R - 1) + (C - 1) + diagonals)

    def edge_copy(dr, dc):
        at = (1 - dr) * 2 + (0 if dc > 0 else 1)
        return pltpu.make_async_remote_copy(
            src_ref=pack, dst_ref=nb.at[at], send_sem=nb_send.at[at], recv_sem=nb_recv.at[at],
            device_id={"row": i + dr, "col": j + dc}, device_id_type=MESH,
        )

    def cond(*terms):
        terms = [t for t in terms if t is not None]
        return functools.reduce(jnp.logical_and, terms)

    def row_copy(down):
        src = rows if down else 2
        dst = 0 if down else rows + 2
        at = 0 if down else 1
        return pltpu.make_async_remote_copy(
            src_ref=ext.at[pl.ds(src, 2), :, pl.ds(0, cols)],
            dst_ref=ext.at[pl.ds(dst, 2), :, pl.ds(0, cols)],
            send_sem=row_send.at[at], recv_sem=row_recv.at[at],
            device_id={"row": i + (1 if down else -1), "col": j}, device_id_type=MESH,
        )

    for dr, ok_r in ups:
        for dc, ok_c in sides:
            @pl.when(cond(ok_r, ok_c))
            def _(dr=dr, dc=dc):
                edge_copy(dr, dc).start()

    @pl.when(has_down)
    def _():
        row_copy(True).start()

    @pl.when(has_up)
    def _():
        row_copy(False).start()

    @pl.when(jnp.logical_not(has_up))
    def _():
        ext[0:2, :, 0:cols] = jnp.zeros((2, n + SUB, cols), jnp.float32)

    @pl.when(jnp.logical_not(has_down))
    def _():
        ext[rows + 2 : rows + 4, :, 0:cols] = jnp.zeros((2, n + SUB, cols), jnp.float32)

    for dr, ok_r in ups:
        for dc, ok_c in sides:
            at = (1 + dr) * 2 + (1 if dc > 0 else 0)
            ok = cond(ok_r, ok_c)

            @pl.when(jnp.logical_not(ok))
            def _(at=at):
                nb[at] = jnp.zeros((2 * SUB, LANES), jnp.float32)

            @pl.when(ok)
            def _(dr=dr, dc=dc):
                edge_copy(-dr, -dc).wait_recv()

    for dr in (0, -1, 1):
        at = (1 + dr) * 2
        merged = [
            jnp.where(
                lane % 4 < 2,
                nb[at, h * SUB : (h + 1) * SUB, :],
                nb[at + 1, h * SUB : (h + 1) * SUB, :],
            )
            for h in range(2)
        ]
        pairs = {
            0: [(r + 2, r) for r in range(rows)],
            -1: [(0, rows - 2), (1, rows - 1)],
            1: [(rows + 2, 0), (rows + 3, 1)],
        }[dr]
        for e, r in pairs:
            for g in range(all_groups):
                which, slot = (0, r * groups + g) if g < groups else (1, r)
                ext[e, g * SUB : (g + 1) * SUB, cols:wide] = pltpu.roll(
                    merged[which], (-(4 * slot + 2)) % LANES, 1
                )

    @pl.when(has_up)
    def _():
        row_copy(True).wait_recv()

    @pl.when(has_down)
    def _():
        row_copy(False).wait_recv()

    def apply(src, e, e_w, g, width):
        at = pl.ds(g * SUB, SUB)
        parts = {}
        for a in (-1, 0, 1):
            v = src[e + a, at, :]
            parts[a, 0] = v[:, :width]
            parts[a, -1] = pltpu.roll(v, 1, 1)[:, :width]
            parts[a, 1] = pltpu.roll(v, wide - 1, 1)[:, :width]
        taps = [
            jnp.broadcast_to(ext[e_w, pl.ds(n + k, 1), 0:width], (SUB, width)) for k in range(SUB)
        ]
        total = functools.reduce(jnp.add, taps) * parts[0, 0]
        for k, offset in enumerate(NEIGHBOURS):
            total = total + taps[k] * parts[offset]
        return total

    def first(e, carry):
        for g in range(groups):
            y1[e - 1, g * SUB : (g + 1) * SUB, :] = apply(ext, e, e, g, wide)
        return carry

    lax.fori_loop(1, rows + 3, first, 0)

    def second(r, carry):
        for g in range(groups):
            y2[r, g * SUB : (g + 1) * SUB, :] = apply(y1, r + 1, r + 2, g, cols)
        return carry

    lax.fori_loop(0, rows, second, 0)

    def gram(load):
        total = jnp.zeros((2 * n, 2 * n), jnp.float32)
        for r in range(rows):
            both = jnp.concatenate(split(load(r)), axis=0)
            total = total + lax.dot_general(both, both, NT, preferred_element_type=jnp.float32)
        half = total[0:n] + total[n : 2 * n]
        return half[:, 0:n] + half[:, n : 2 * n]

    gram_1 = gram(lambda r: y1[r + 1, :, 0:cols])
    gram_2 = gram(lambda r: y2[r])
    grams = jnp.concatenate([gram_1, gram_2], axis=1) * (1.0 / (rows * cols * R * C))
    compact = jnp.concatenate([grams[0 : n // 2], grams[n // 2 : n]], axis=1)

    def exchange(value, sent, held, me, count, axis, send_sems, recv_sems):
        sent[...] = value
        held[me] = value

        def target(d):
            peer = lax.rem(me + d, count)
            return {"row": peer, "col": j} if axis == "row" else {"row": i, "col": peer}

        copies = [
            pltpu.make_async_remote_copy(
                src_ref=sent, dst_ref=held.at[me], send_sem=send_sems.at[d - 1],
                recv_sem=recv_sems.at[me], device_id=target(d), device_id_type=MESH,
            )
            for d in range(1, count)
        ]
        for copy in copies:
            copy.start()
        for d in range(1, count):
            peer = lax.rem(me + d, count)
            pltpu.make_async_remote_copy(
                src_ref=sent, dst_ref=held.at[peer], send_sem=send_sems.at[d - 1],
                recv_sem=recv_sems.at[peer], device_id=target(d), device_id_type=MESH,
            ).wait_recv()
        total = held[0]
        for at in range(1, count):
            total = total + held[at]
        return total, copies

    in_row, row_copies = exchange(compact, gsend1, gr, i, R, "row", gr_send, gr_recv)
    in_all, col_copies = exchange(in_row, gsend2, gc, j, C, "col", gc_send, gc_recv)

    whole = jnp.concatenate([in_all, pltpu.roll(in_all, LANES // 2, 1)], axis=0)
    later = pltpu.roll(whole, n, 1)
    sub_n = lax.broadcasted_iota(jnp.int32, (n, LANES), 0)
    lane_n = lax.broadcasted_iota(jnp.int32, (n, LANES), 1)
    quarter = lane_n // n
    eye = (lane_n % n == sub_n).astype(jnp.float32)
    table = jnp.where(quarter == 0, whole, jnp.where(quarter == 2, later, eye))
    blocks = [table[g * SUB : (g + 1) * SUB] for g in range(groups)]
    sub = lax.broadcasted_iota(jnp.int32, (SUB, LANES), 0)
    low_half = lane < LANES // 2
    for p in range(n):
        home = p // SUB
        row = jnp.broadcast_to(blocks[home][p % SUB : p % SUB + 1, :], (SUB, LANES))
        pivot = jnp.where(low_half, row[:, p : p + 1], row[:, 2 * n + p : 2 * n + p + 1])
        scaled = row / pivot
        for g in range(home, groups):
            mine = blocks[g]
            factor = jnp.where(low_half, mine[:, p : p + 1], mine[:, 2 * n + p : 2 * n + p + 1])
            update = factor * scaled
            if g == home:
                update = jnp.where(sub > p % SUB, update, 0.0)
            blocks[g] = mine - update
    table = jnp.concatenate(blocks, axis=0)
    on_diagonal = lane_n % n == sub_n
    diag_1 = jnp.sum(
        jnp.where(jnp.logical_and(on_diagonal, quarter == 0), table, 0.0), axis=1, keepdims=True
    )
    diag_2 = jnp.sum(
        jnp.where(jnp.logical_and(on_diagonal, quarter == 2), table, 0.0), axis=1, keepdims=True
    )
    table = table / jnp.sqrt(jnp.where(quarter < 2, diag_1, diag_2))
    inverse_1 = table[:, n : 2 * n]
    upper_2 = table[:, 2 * n : 3 * n]
    inverse_2 = table[:, 3 * n : 4 * n]
    row_at = lax.broadcasted_iota(jnp.int32, (n, n), 0)
    col_at = lax.broadcasted_iota(jnp.int32, (n, n), 1)
    upper_2 = jnp.where(col_at >= row_at, upper_2, 0.0)
    last = lax.dot_general(
        upper_2, inverse_1, NT, precision=HIGHEST, preferred_element_type=jnp.float32
    )
    fac_ref[...] = jnp.where(col_at >= row_at, last, 0.0)

    inv_hi, inv_lo = split(inverse_2)
    left = jnp.concatenate([inv_hi, inv_lo, inv_hi], axis=1)
    stores = []
    for t0 in range(0, tiles, 2):
        for r in range(rows):
            hi, lo = split(y2[r, :, t0 * LANES : (t0 + 2) * LANES])
            right = jnp.concatenate([hi, hi, lo], axis=0)
            solved = jnp.dot(left, right, preferred_element_type=jnp.float32)
            for t in range(2):
                for g in range(groups):
                    staged[t0 + t, pl.ds(g * SUB * rows + r, SUB, stride=rows), :] = solved[
                        g * SUB : (g + 1) * SUB, t * LANES : (t + 1) * LANES
                    ]
        for t in range(t0, t0 + 2):
            stores.append(pltpu.make_async_copy(
                staged.at[t], out_ref.at[:, pl.ds(t * LANES, LANES)], store_sem.at[t]
            ))
            stores[-1].start()
    for store in stores:
        store.wait()

    for dr, ok_r in ups:
        for dc, ok_c in sides:
            @pl.when(cond(ok_r, ok_c))
            def _(dr=dr, dc=dc):
                edge_copy(dr, dc).wait_send()

    @pl.when(has_down)
    def _():
        row_copy(True).wait_send()

    @pl.when(has_up)
    def _():
        row_copy(False).wait_send()

    for copy in row_copies + col_copies:
        copy.wait_send()


def on_device(sketch, weights):
    n, rows, cols = sketch.shape
    R, C = lax.axis_size("row"), lax.axis_size("col")
    dma = pltpu.SemaphoreType.DMA
    f32 = jnp.float32
    basis, factor = pl.pallas_call(
        functools.partial(kernel, n, rows, cols, R, C),
        out_shape=(
            jax.ShapeDtypeStruct((n * rows, cols), f32),
            jax.ShapeDtypeStruct((n, n), f32),
        ),
        in_specs=[pl.BlockSpec(memory_space=pl.ANY)] * 2,
        out_specs=(
            pl.BlockSpec(memory_space=pl.ANY),
            pl.BlockSpec(memory_space=pltpu.VMEM),
        ),
        scratch_shapes=[
            pltpu.VMEM((cols // LANES, n * rows, LANES), f32),
            pltpu.VMEM((cols // LANES, SUB * rows, LANES), f32),
            pltpu.VMEM((cols // LANES, n * rows, LANES), f32),
            pltpu.VMEM((rows + 4, n + SUB, cols + LANES), f32),
            pltpu.VMEM((rows + 2, n, cols + LANES), f32),
            pltpu.VMEM((rows, n, cols), f32),
            pltpu.VMEM((2 * SUB, LANES), f32),
            pltpu.VMEM((6, 2 * SUB, LANES), f32),
            pltpu.VMEM((R, n // 2, LANES), f32),
            pltpu.VMEM((C, n // 2, LANES), f32),
            pltpu.VMEM((n // 2, LANES), f32),
            pltpu.VMEM((n // 2, LANES), f32),
            dma((2, cols // LANES)), dma((cols // LANES,)), dma((2,)), dma((2,)), dma((6,)), dma((6,)),
            dma((R,)), dma((R,)), dma((C,)), dma((C,)),
        ],
        compiler_params=pltpu.CompilerParams(
            collective_id=0, has_side_effects=True, vmem_limit_bytes=32 * 1024 * 1024
        ),
    )(sketch.reshape(n * rows, cols), weights.reshape(SUB * rows, cols))
    return basis.reshape(n, rows, cols), factor


def solution(mesh):
    return jax.shard_map(
        on_device,
        mesh=mesh,
        in_specs=(P(None, ("sec", "row"), "col"), P(None, ("sec", "row"), "col")),
        out_specs=(P(None, ("sec", "row"), "col"), P("sec", None)),
        check_vma=False,
    )
```

time: 179 us -> 28.4 us (0.16)
  blocking collectives: 117 us -> 0 us
  Pallas kernels: 0 us -> 24.2 us
  starting transfers between devices: 19.8 us -> 0 us
  other arithmetic: 16.3 us -> 0 us
  waiting for transfers between devices: 12.8 us -> 0 us
  matrix products: 5.25 us -> 0 us
  local copies, waits for them, and re-layouts: 6.29 us -> 3.34 us
    psum x2 -> x0, blocking collectives: 117 us -> none  [factorize(): summed = lax.psum(gram_local, ('row', 'col'))]
    pallas_call x0 -> x1, Pallas kernels: none -> 24.2 us  [on_device(): pl.pallas_call(functools.partial(kernel, n, rows, cols, R, C), out_shape=...]
    ppermute x8 -> x0, starting transfers between devices: 19.8 us -> none  [the longest x4 14.5 us: padded_2(): lax.ppermute(lax.slice_in_dim(block, block.shape[dim] - width, None, axis...]
    ppermute x8 -> x0, waiting for transfers between devices: 12.8 us -> none  [the longest x4 8.38 us: padded_2(): lax.ppermute(lax.slice_in_dim(block, 0, width, axis=dim), axis, backward)]
    another operation x9 -> x0, other arithmetic: 12.7 us -> none  [the longest x6 7.19 us: factorize(): return jnp.linalg.cholesky(summed)]
    dot_general x2 -> x0, matrix products: 2.82 us -> none  [factorize(): jnp.dot(flattened, flattened.T, precision=lax.Precision.HIGHEST)]
    slice x3 -> x0, local copies, waits for them, and re-layouts: 2.57 us -> none  [the longest x1 1.38 us: padded_2(): lax.slice_in_dim(block, 0, width, axis=dim)]
    another operation x2 -> x0, matrix products: 2.43 us -> none  [solve_planes(): jax.scipy.linalg.solve_triangular(lower_tri, image_vals.reshape(columns,...]
  transfers between devices with their start and end apart: 8 -> 0, of which waited for: 4 -> 0; matrix products, arithmetic and copies ran while one was open for 2% -> 0% of each run, Pallas kernels for 0% -> 0%
where the time goes in v1:
time: 28.4 us; the launch traced here: 28.2 us
  Pallas kernels  24.2 us (85%)
  local copies, waits for them, and re-layouts  3.34 us (12%)
  between operations  0.65 us (2%)
    pallas_call x1, Pallas kernels, on_device(): pl.pallas_call(functools.partial(kernel, n, rows, cols, R, C), out_shape=...  24.2 us
    unnamed x6, local copies, waits for them, and re-layouts  3.34 us

profile of v1, /device:TPU:0, one launch (start us, length us, event | category | flops | bytes accessed | tf_op | source)
XLA Modules:
  0.0 28.2 jit_solution(14482448146317897298)
XLA Ops:
  0.6 0.0 copy-start
  0.6 1.0 %copy-done = f32[32,8,512]{2,1,0:T(8,128)S(1)} copy-done((f32[32,8,512]{2,1,0:T(8,128)S(1)}, f32[32,8,512]{2,1,0:T(8,128)}, u32[]{:S(2)}) %copy-start) | copy-done | bytes 524312
  1.7 0.0 copy-start.1
  1.7 0.9 %copy-done.1 = f32[8,8,512]{2,1,0:T(8,128)S(1)} copy-done((f32[8,8,512]{2,1,0:T(8,128)S(1)}, f32[8,8,512]{2,1,0:T(8,128)}, u32[]{:S(2)}) %copy-start.1) | copy-done | bytes 131096
  2.6 24.2 %shard_map.41 = (f32[256,512]{1,0:T(8,128)S(1)}, f32[32,32]{1,0:T(8,128)S(1)}) custom-call(f32[256,512]{1,0:T(8,128)S(1)} %bitcast.3, f32[64,512]{1,0:T(8,128)S(1)} %bitcast.5), custom_call_target="tpu_custom_call" | custom-call | tf_op jit(solution)/shard_map/pallas_call | solution.py:350
  26.8 0.8 %copy.6 = f32[32,8,512]{2,1,0:T(8,128)} copy(f32[32,8,512]{2,1,0:T(8,128)S(1)} %bitcast.4) | data formatting | bytes 1048576
  27.6 0.6 %copy.7 = f32[32,32]{1,0:T(8,128)} copy(f32[32,32]{1,0:T(8,128)S(1)} %get-tuple-element.9) | data formatting | bytes 8192
Async XLA Ops:
  0.6 1.0 %copy-start = (f32[32,8,512]{2,1,0:T(8,128)S(1)}, f32[32,8,512]{2,1,0:T(8,128)}, u32[]{:S(2)}) copy-start(f32[32,8,512]{2,1,0:T(8,128)} %param.2) | copy-start | bytes 1572868
  1.7 0.9 %copy-start.1 = (f32[8,8,512]{2,1,0:T(8,128)S(1)}, f32[8,8,512]{2,1,0:T(8,128)}, u32[]{:S(2)}) copy-start(f32[8,8,512]{2,1,0:T(8,128)} %param.3) | copy-start | bytes 393220

commit v2 on v1

v2 whole, which is shorter than its diff:
```python
import functools

import jax
import jax.numpy as jnp
from jax import lax
from jax.experimental import pallas as pl
from jax.experimental.pallas import tpu as pltpu
from jax.sharding import PartitionSpec as P

LANES = 128
SUB = 8
NEIGHBOURS = ((-1, -1), (-1, 0), (-1, 1), (0, -1), (0, 1), (1, -1), (1, 0), (1, 1))
MESH = pl.DeviceIdType.MESH
NT = (((1,), (1,)), ((), ()))
HIGHEST = lax.Precision.HIGHEST


def split(x):
    hi = x.astype(jnp.bfloat16)
    lo = (x - hi.astype(jnp.float32)).astype(jnp.bfloat16)
    return hi, lo


def kernel(
    n, rows, cols, R, C,
    sk_hbm, w_hbm, out_ref, fac_ref,
    raw, wraw, staged, ext, ext_l, ext_r, y1, y1_l, y1_r, y2, pack, nb, held_row, held_col, sent,
    load_sem, store_sem, row_send, row_recv, nb_send, nb_recv, gr_send, gr_recv, gc_send, gc_recv,
):
    groups = n // SUB
    all_groups = groups + 1
    wide = cols + LANES
    i = lax.axis_index("row")
    j = lax.axis_index("col")
    has_up, has_down = i > 0, i < R - 1
    has_left, has_right = j > 0, j < C - 1

    tiles = cols // LANES
    loads = []
    for t in range(tiles):
        across = pl.ds(t * LANES, LANES)
        loads.append(pltpu.make_async_copy(sk_hbm.at[:, across], raw.at[t], load_sem.at[0, t]))
        loads.append(pltpu.make_async_copy(w_hbm.at[:, across], wraw.at[t], load_sem.at[1, t]))
    for load in loads:
        load.start()

    barrier = pltpu.get_barrier_semaphore()
    for d in range(1, R):
        pl.semaphore_signal(
            barrier, inc=1, device_id={"row": lax.rem(i + d, R), "col": j}, device_id_type=MESH
        )
    for d in range(1, C):
        pl.semaphore_signal(
            barrier, inc=1, device_id={"row": i, "col": lax.rem(j + d, C)}, device_id_type=MESH
        )
    ups = ((-1, has_up), (0, None), (1, has_down))
    sides = ((-1, has_left), (1, has_right))
    for dr, ok_r in ups:
        for dc, ok_c in sides:
            if dr != 0:
                @pl.when(jnp.logical_and(ok_r, ok_c))
                def _(dr=dr, dc=dc):
                    pl.semaphore_signal(
                        barrier, inc=1, device_id={"row": i + dr, "col": j + dc},
                        device_id_type=MESH,
                    )
    diagonals = (has_up.astype(jnp.int32) + has_down.astype(jnp.int32)) * (
        has_left.astype(jnp.int32) + has_right.astype(jnp.int32)
    )

    lane = lax.broadcasted_iota(jnp.int32, (SUB, LANES), 1)

    def relayout(r):
        for t in range(tiles):
            across = slice(t * LANES, (t + 1) * LANES)
            for g in range(groups):
                ext[r + 2, g * SUB : (g + 1) * SUB, across] = raw[
                    t, pl.ds(g * SUB * rows + r, SUB, stride=rows), :
                ]
            ext[r + 2, n : n + SUB, across] = wraw[t, pl.ds(r, SUB, stride=rows), :]

    for load in loads:
        load.wait()
    for r in range(rows):
        relayout(r)

    def edge_copy(dr, dc):
        at = (1 - dr) * 2 + (0 if dc > 0 else 1)
        return pltpu.make_async_remote_copy(
            src_ref=pack, dst_ref=nb.at[at], send_sem=nb_send.at[at], recv_sem=nb_recv.at[at],
            device_id={"row": i + dr, "col": j + dc}, device_id_type=MESH,
        )

    def cond(*terms):
        terms = [t for t in terms if t is not None]
        return functools.reduce(jnp.logical_and, terms)

    def row_copy(down):
        src = rows if down else 2
        dst = 0 if down else rows + 2
        at = 0 if down else 1
        return pltpu.make_async_remote_copy(
            src_ref=ext.at[pl.ds(src, 2), :, pl.ds(0, cols)],
            dst_ref=ext.at[pl.ds(dst, 2), :, pl.ds(0, cols)],
            send_sem=row_send.at[at], recv_sem=row_recv.at[at],
            device_id={"row": i + (1 if down else -1), "col": j}, device_id_type=MESH,
        )

    pl.semaphore_wait(barrier, (R - 1) + (C - 1) + diagonals)

    @pl.when(has_down)
    def _():
        row_copy(True).start()

    @pl.when(has_up)
    def _():
        row_copy(False).start()

    packed = [jnp.zeros((SUB, LANES), jnp.float32), jnp.zeros((SUB, LANES), jnp.float32)]
    for r in range(rows):
        for g in range(all_groups):
            which, slot = (0, r * groups + g) if g < groups else (1, r)
            edge = jnp.where(
                lane < LANES // 2,
                ext[r + 2, g * SUB : (g + 1) * SUB, 0:LANES],
                ext[r + 2, g * SUB : (g + 1) * SUB, cols - LANES : cols],
            )
            moved = pltpu.roll(edge, (4 * slot + 2) % LANES, 1)
            packed[which] = jnp.where(lane // 4 == slot, moved, packed[which])
    pack[0:SUB, :] = packed[0]
    pack[SUB : 2 * SUB, :] = packed[1]

    for dr, ok_r in (ups[1], ups[0], ups[2]):
        for dc, ok_c in sides:
            @pl.when(cond(ok_r, ok_c))
            def _(dr=dr, dc=dc):
                edge_copy(dr, dc).start()

    @pl.when(jnp.logical_not(has_up))
    def _():
        ext[0:2, :, 0:cols] = jnp.zeros((2, n + SUB, cols), jnp.float32)

    @pl.when(jnp.logical_not(has_down))
    def _():
        ext[rows + 2 : rows + 4, :, 0:cols] = jnp.zeros((2, n + SUB, cols), jnp.float32)

    def receive_edges(dr, ok_r):
        for dc, ok_c in sides:
            at = (1 + dr) * 2 + (1 if dc > 0 else 0)
            ok = cond(ok_r, ok_c)

            @pl.when(jnp.logical_not(ok))
            def _(at=at):
                nb[at] = jnp.zeros((2 * SUB, LANES), jnp.float32)

            @pl.when(ok)
            def _(dr=dr, dc=dc):
                edge_copy(-dr, -dc).wait_recv()

        at = (1 + dr) * 2
        merged = [
            jnp.where(
                lane % 4 < 2,
                nb[at, h * SUB : (h + 1) * SUB, :],
                nb[at + 1, h * SUB : (h + 1) * SUB, :],
            )
            for h in range(2)
        ]
        pairs = {
            0: [(r + 2, r) for r in range(rows)],
            -1: [(0, rows - 2), (1, rows - 1)],
            1: [(rows + 2, 0), (rows + 3, 1)],
        }[dr]
        for e, r in pairs:
            for g in range(all_groups):
                which, slot = (0, r * groups + g) if g < groups else (1, r)
                ext[e, g * SUB : (g + 1) * SUB, cols:wide] = pltpu.roll(
                    merged[which], (-(4 * slot + 2)) % LANES, 1
                )

    def rotate(src, left, right, first, last):
        def body(e, carry):
            for g in range(groups):
                at = pl.ds(g * SUB, SUB)
                v = src[e, at, :]
                left[e, at, :] = pltpu.roll(v, 1, 1)[:, : left.shape[2]]
                right[e, at, :] = pltpu.roll(v, wide - 1, 1)[:, : right.shape[2]]
            return carry

        lax.fori_loop(first, last, body, 0)

    def apply(srcs, dst, e_first, e_last, w_shift, dst_shift, lane_tiles):
        def body(t, carry):
            across = pl.ds(pl.multiple_of(t * LANES, LANES), LANES)
            window = {}

            def load(e):
                for g in range(groups):
                    for b, src in zip((-1, 0, 1), srcs):
                        window[e, g, b] = src[e, pl.ds(g * SUB, SUB), across]

            load(e_first - 1)
            load(e_first)
            for e in range(e_first, e_last):
                load(e + 1)
                taps = [
                    jnp.broadcast_to(ext[e + w_shift, pl.ds(n + k, 1), across], (SUB, LANES))
                    for k in range(SUB)
                ]
                degree = functools.reduce(jnp.add, taps)
                for g in range(groups):
                    total = degree * window[e, g, 0]
                    for k, (da, db) in enumerate(NEIGHBOURS):
                        total = total + taps[k] * window[e + da, g, db]
                    dst[e + dst_shift, pl.ds(g * SUB, SUB), across] = total
            return carry

        lax.fori_loop(0, lane_tiles, body, 0)

    wide_srcs = (ext_l, ext, ext_r)
    receive_edges(0, None)
    rotate(ext, ext_l, ext_r, 2, rows + 2)
    apply(wide_srcs, y1, 3, rows + 1, 0, -1, tiles + 1)
    receive_edges(-1, has_up)
    receive_edges(1, has_down)

    @pl.when(has_up)
    def _():
        row_copy(True).wait_recv()

    @pl.when(has_down)
    def _():
        row_copy(False).wait_recv()

    rotate(ext, ext_l, ext_r, 0, 2)
    rotate(ext, ext_l, ext_r, rows + 2, rows + 4)
    apply(wide_srcs, y1, 1, 3, 0, -1, tiles + 1)
    apply(wide_srcs, y1, rows + 1, rows + 3, 0, -1, tiles + 1)

    scale = 1.0 / (rows * cols * R * C)

    def gram(load):
        total = jnp.zeros((2 * n, 2 * n), jnp.float32)
        for r in range(rows):
            both = jnp.concatenate(split(load(r)), axis=0)
            total = total + lax.dot_general(both, both, NT, preferred_element_type=jnp.float32)
        half = total[0:n] + total[n : 2 * n]
        square = (half[:, 0:n] + half[:, n : 2 * n]) * scale
        return jnp.concatenate([square[g * SUB : (g + 1) * SUB] for g in range(groups)], axis=1)

    def gather_copies(which, axis, receiving):
        held, me, count, send_sems, recv_sems = (
            (held_row, i, R, gr_send, gr_recv) if axis == "row" else (held_col, j, C, gc_send, gc_recv)
        )
        at = which * 2 + (0 if axis == "row" else 1)
        copies = []
        for d in range(1, count):
            peer = lax.rem(me + d, count)
            slot = peer if receiving else me
            copies.append(pltpu.make_async_remote_copy(
                src_ref=sent.at[at], dst_ref=held.at[which, slot],
                send_sem=send_sems.at[which, d - 1], recv_sem=recv_sems.at[which, slot],
                device_id={"row": peer, "col": j} if axis == "row" else {"row": i, "col": peer},
                device_id_type=MESH,
            ))
        return copies

    def spread(which, axis, value):
        sent[which * 2 + (0 if axis == "row" else 1)] = value
        if axis == "row":
            held_row[which, i] = value
        else:
            held_col[which, j] = value
        for copy in gather_copies(which, axis, False):
            copy.start()

    def collect(which, axis):
        for copy in gather_copies(which, axis, True):
            copy.wait_recv()
        held, count = (held_row, R) if axis == "row" else (held_col, C)
        total = held[which, 0]
        for at in range(1, count):
            total = total + held[which, at]
        return total

    sub = lax.broadcasted_iota(jnp.int32, (SUB, LANES), 0)

    def eliminate(tile, step=4):
        blocks = []
        for g in range(groups):
            mine = tile if g == 0 else pltpu.roll(tile, LANES - g * n, 1)
            eye = (lane - n == sub + g * SUB).astype(jnp.float32)
            blocks.append(jnp.where(lane < n, mine, eye))
        for p in range(0, n, step):
            home, base = p // SUB, p % SUB
            line = [
                jnp.broadcast_to(blocks[home][base + q : base + q + 1, :], (SUB, LANES))
                for q in range(step)
            ]
            column = {
                (s, g): jnp.broadcast_to(blocks[g][:, p + s : p + s + 1], (SUB, LANES))
                for g in range(home, groups)
                for s in range(step)
            }
            corner = {
                (q, s): jnp.broadcast_to(column[s, home][base + q : base + q + 1, :], (SUB, LANES))
                for q in range(step)
                for s in range(q, step)
            }
            scaled = []
            for q in range(step):
                over = 1.0 / corner[q, q]
                scaled.append(line[q] * over)
                ratio = {s: corner[q, s] * over for s in range(q + 1, step)}
                for s in range(q + 1, step):
                    line[s] = line[s] - ratio[s] * line[q]
                    for t in range(s, step):
                        corner[s, t] = corner[s, t] - ratio[s] * corner[q, t]
                    for g in range(home, groups):
                        column[s, g] = column[s, g] - ratio[s] * column[q, g]
            for g in range(home, groups):
                if g == home and base + step == SUB:
                    continue
                update = column[0, g] * scaled[0]
                for q in range(1, step):
                    update = update + column[q, g] * scaled[q]
                if g == home:
                    update = jnp.where(sub >= base + step, update, 0.0)
                blocks[g] = blocks[g] - update
            for q in range(step):
                done = line[q] * (1.0 / jnp.sqrt(corner[q, q]))
                blocks[home] = jnp.where(sub == base + q, done, blocks[home])
        return jnp.concatenate(blocks, axis=0)

    spread(0, "row", gram(lambda r: y1[r + 1, :, 0:cols]))
    rotate(y1, y1_l, y1_r, 0, rows + 2)
    apply((y1_l, y1, y1_r), y2, 1, rows + 1, 1, -1, tiles)
    second = gram(lambda r: y2[r])
    spread(1, "row", second)
    spread(0, "col", collect(0, "row"))
    spread(1, "col", collect(1, "row"))
    table_1 = eliminate(collect(0, "col"))
    table_2 = eliminate(collect(1, "col"))

    inverse_1 = table_1[:, n : 2 * n]
    upper_2 = table_2[:, 0:n]
    inverse_2 = table_2[:, n : 2 * n]
    row_at = lax.broadcasted_iota(jnp.int32, (n, n), 0)
    col_at = lax.broadcasted_iota(jnp.int32, (n, n), 1)
    upper_2 = jnp.where(col_at >= row_at, upper_2, 0.0)
    last = lax.dot_general(
        upper_2, inverse_1, NT, precision=HIGHEST, preferred_element_type=jnp.float32
    )
    fac_ref[...] = jnp.where(col_at >= row_at, last, 0.0)

    inv_hi, inv_lo = split(inverse_2)
    left = jnp.concatenate([inv_hi, inv_lo, inv_hi], axis=1)
    stores = []
    for t0 in range(0, tiles, 2):
        for r in range(rows):
            hi, lo = split(y2[r, :, t0 * LANES : (t0 + 2) * LANES])
            right = jnp.concatenate([hi, hi, lo], axis=0)
            solved = jnp.dot(left, right, preferred_element_type=jnp.float32)
            for t in range(2):
                for g in range(groups):
                    staged[t0 + t, pl.ds(g * SUB * rows + r, SUB, stride=rows), :] = solved[
                        g * SUB : (g + 1) * SUB, t * LANES : (t + 1) * LANES
                    ]
        for t in range(t0, t0 + 2):
            stores.append(pltpu.make_async_copy(
                staged.at[t], out_ref.at[:, pl.ds(t * LANES, LANES)], store_sem.at[t]
            ))
            stores[-1].start()
    for store in stores:
        store.wait()

    for dr, ok_r in ups:
        for dc, ok_c in sides:
            @pl.when(cond(ok_r, ok_c))
            def _(dr=dr, dc=dc):
                edge_copy(dr, dc).wait_send()

    @pl.when(has_down)
    def _():
        row_copy(True).wait_send()

    @pl.when(has_up)
    def _():
        row_copy(False).wait_send()

    for which in range(2):
        for axis in ("row", "col"):
            for copy in gather_copies(which, axis, False):
                copy.wait_send()


def on_device(sketch, weights):
    n, rows, cols = sketch.shape
    R, C = lax.axis_size("row"), lax.axis_size("col")
    dma = pltpu.SemaphoreType.DMA
    f32 = jnp.float32
    basis, factor = pl.pallas_call(
        functools.partial(kernel, n, rows, cols, R, C),
        out_shape=(
            jax.ShapeDtypeStruct((n * rows, cols), f32),
            jax.ShapeDtypeStruct((n, n), f32),
        ),
        in_specs=[pl.BlockSpec(memory_space=pltpu.HBM)] * 2,
        out_specs=(
            pl.BlockSpec(memory_space=pl.ANY),
            pl.BlockSpec(memory_space=pltpu.VMEM),
        ),
        scratch_shapes=[
            pltpu.VMEM((cols // LANES, n * rows, LANES), f32),
            pltpu.VMEM((cols // LANES, SUB * rows, LANES), f32),
            pltpu.VMEM((cols // LANES, n * rows, LANES), f32),
            pltpu.VMEM((rows + 4, n + SUB, cols + LANES), f32),
            pltpu.VMEM((rows + 4, n, cols + LANES), f32),
            pltpu.VMEM((rows + 4, n, cols + LANES), f32),
            pltpu.VMEM((rows + 2, n, cols + LANES), f32),
            pltpu.VMEM((rows + 2, n, cols), f32),
            pltpu.VMEM((rows + 2, n, cols), f32),
            pltpu.VMEM((rows, n, cols), f32),
            pltpu.VMEM((2 * SUB, LANES), f32),
            pltpu.VMEM((6, 2 * SUB, LANES), f32),
            pltpu.VMEM((2, R, SUB, LANES), f32),
            pltpu.VMEM((2, C, SUB, LANES), f32),
            pltpu.VMEM((4, SUB, LANES), f32),
            dma((2, cols // LANES)), dma((cols // LANES,)), dma((2,)), dma((2,)), dma((6,)), dma((6,)),
            dma((2, R)), dma((2, R)), dma((2, C)), dma((2, C)),
        ],
        compiler_params=pltpu.CompilerParams(
            collective_id=0, has_side_effects=True, vmem_limit_bytes=32 * 1024 * 1024
        ),
    )(sketch.reshape(n * rows, cols), weights.reshape(SUB * rows, cols))
    return basis.reshape(n, rows, cols), factor


def solution(mesh):
    return jax.shard_map(
        on_device,
        mesh=mesh,
        in_specs=(P(None, ("sec", "row"), "col"), P(None, ("sec", "row"), "col")),
        out_specs=(P(None, ("sec", "row"), "col"), P("sec", None)),
        check_vma=False,
    )
```

time: 28.4 us -> 25.1 us (0.88)
  Pallas kernels: 24.2 us -> 20.9 us
    pallas_call x1, Pallas kernels: 24.2 us -> 20.9 us  [on_device(): pl.pallas_call(functools.partial(kernel, n, rows, cols, R, C), out_shape=...]
where the time goes in v2:
time: 25.1 us; the launch traced here: 24.9 us
  Pallas kernels  20.9 us (83%)
  local copies, waits for them, and re-layouts  3.34 us (13%)
  between operations  0.65 us (3%)
    pallas_call x1, Pallas kernels, on_device(): pl.pallas_call(functools.partial(kernel, n, rows, cols, R, C), out_shape=...  20.9 us
    unnamed x6, local copies, waits for them, and re-layouts  3.34 us

profile of v2, /device:TPU:0, one launch (start us, length us, event | category | flops | bytes accessed | tf_op | source)
XLA Modules:
  0.0 24.9 jit_solution(4522723939200749707)
XLA Ops:
  0.6 0.0 copy-start
  0.6 1.0 %copy-done = f32[32,8,512]{2,1,0:T(8,128)S(1)} copy-done((f32[32,8,512]{2,1,0:T(8,128)S(1)}, f32[32,8,512]{2,1,0:T(8,128)}, u32[]{:S(2)}) %copy-start) | copy-done | bytes 524312
  1.7 0.0 copy-start.1
  1.7 0.9 %copy-done.1 = f32[8,8,512]{2,1,0:T(8,128)S(1)} copy-done((f32[8,8,512]{2,1,0:T(8,128)S(1)}, f32[8,8,512]{2,1,0:T(8,128)}, u32[]{:S(2)}) %copy-start.1) | copy-done | bytes 131096
  2.6 20.9 %shard_map.41 = (f32[256,512]{1,0:T(8,128)S(1)}, f32[32,32]{1,0:T(8,128)S(1)}) custom-call(f32[256,512]{1,0:T(8,128)S(1)} %bitcast.3, f32[64,512]{1,0:T(8,128)S(1)} %bitcast.5), custom_call_target="tpu_custom_call" | custom-call | tf_op jit(solution)/shard_map/pallas_call | solution.py:402
  23.5 0.8 %copy.6 = f32[32,8,512]{2,1,0:T(8,128)} copy(f32[32,8,512]{2,1,0:T(8,128)S(1)} %bitcast.4) | data formatting | bytes 1048576
  24.3 0.6 %copy.7 = f32[32,32]{1,0:T(8,128)} copy(f32[32,32]{1,0:T(8,128)S(1)} %get-tuple-element.9) | data formatting | bytes 8192
Async XLA Ops:
  0.6 1.0 %copy-start = (f32[32,8,512]{2,1,0:T(8,128)S(1)}, f32[32,8,512]{2,1,0:T(8,128)}, u32[]{:S(2)}) copy-start(f32[32,8,512]{2,1,0:T(8,128)} %param.2) | copy-start | bytes 1572868
  1.7 0.9 %copy-start.1 = (f32[8,8,512]{2,1,0:T(8,128)S(1)}, f32[8,8,512]{2,1,0:T(8,128)}, u32[]{:S(2)}) copy-start(f32[8,8,512]{2,1,0:T(8,128)} %param.3) | copy-start | bytes 393220

commit v3 on v2

--- a/solution.py
+++ b/solution.py
@@ -22,10 +22,10 @@
 
 
 def kernel(
-    n, rows, cols, R, C,
+    n, rows, cols, R, C, stages,
     sk_hbm, w_hbm, out_ref, fac_ref,
-    raw, wraw, staged, ext, ext_l, ext_r, y1, y1_l, y1_r, y2, pack, nb, held_row, held_col, sent,
-    load_sem, store_sem, row_send, row_recv, nb_send, nb_recv, gr_send, gr_recv, gc_send, gc_recv,
+    raw, wraw, staged, ext, ext_l, ext_r, y1, y1_l, y1_r, y2, pack, nb, held, sent,
+    load_sem, store_sem, row_send, row_recv, nb_send, nb_recv, gather_send, gather_recv,
 ):
     groups = n // SUB
     all_groups = groups + 1
@@ -45,26 +45,26 @@
         load.start()
 
     barrier = pltpu.get_barrier_semaphore()
-    for d in range(1, R):
-        pl.semaphore_signal(
-            barrier, inc=1, device_id={"row": lax.rem(i + d, R), "col": j}, device_id_type=MESH
-        )
-    for d in range(1, C):
-        pl.semaphore_signal(
-            barrier, inc=1, device_id={"row": i, "col": lax.rem(j + d, C)}, device_id_type=MESH
-        )
+    if len(stages) == 1:
+        peers = [lax.rem(i * C + j + d, R * C) for d in range(1, R * C)]
+        partners = [(lax.div(peer, C), lax.rem(peer, C)) for peer in peers]
+    else:
+        partners = [(lax.rem(i + d, R), j) for d in range(1, R)]
+        partners += [(i, lax.rem(j + d, C)) for d in range(1, C)]
+    for r, c in partners:
+        pl.semaphore_signal(barrier, inc=1, device_id={"row": r, "col": c}, device_id_type=MESH)
     ups = ((-1, has_up), (0, None), (1, has_down))
     sides = ((-1, has_left), (1, has_right))
     for dr, ok_r in ups:
         for dc, ok_c in sides:
-            if dr != 0:
+            if dr != 0 and len(stages) > 1:
                 @pl.when(jnp.logical_and(ok_r, ok_c))
                 def _(dr=dr, dc=dc):
                     pl.semaphore_signal(
                         barrier, inc=1, device_id={"row": i + dr, "col": j + dc},
                         device_id_type=MESH,
                     )
-    diagonals = (has_up.astype(jnp.int32) + has_down.astype(jnp.int32)) * (
+    diagonals = 0 if len(stages) == 1 else (has_up.astype(jnp.int32) + has_down.astype(jnp.int32)) * (
         has_left.astype(jnp.int32) + has_right.astype(jnp.int32)
     )
 
@@ -106,7 +106,7 @@
             device_id={"row": i + (1 if down else -1), "col": j}, device_id_type=MESH,
         )
 
-    pl.semaphore_wait(barrier, (R - 1) + (C - 1) + diagonals)
+    pl.semaphore_wait(barrier, len(partners) + diagonals)
 
     @pl.when(has_down)
     def _():
@@ -248,40 +248,41 @@
         square = (half[:, 0:n] + half[:, n : 2 * n]) * scale
         return jnp.concatenate([square[g * SUB : (g + 1) * SUB] for g in range(groups)], axis=1)
 
-    def gather_copies(which, axis, receiving):
-        held, me, count, send_sems, recv_sems = (
-            (held_row, i, R, gr_send, gr_recv) if axis == "row" else (held_col, j, C, gc_send, gc_recv)
-        )
-        at = which * 2 + (0 if axis == "row" else 1)
+    def gather_copies(which, stage, receiving):
+        axes, count = stages[stage]
+        me = {"row": i, "col": j, "both": i * C + j}[axes]
         copies = []
         for d in range(1, count):
             peer = lax.rem(me + d, count)
             slot = peer if receiving else me
+            target = {
+                "row": {"row": peer, "col": j},
+                "col": {"row": i, "col": peer},
+                "both": {"row": lax.div(peer, C), "col": lax.rem(peer, C)},
+            }[axes]
             copies.append(pltpu.make_async_remote_copy(
-                src_ref=sent.at[at], dst_ref=held.at[which, slot],
-                send_sem=send_sems.at[which, d - 1], recv_sem=recv_sems.at[which, slot],
-                device_id={"row": peer, "col": j} if axis == "row" else {"row": i, "col": peer},
-                device_id_type=MESH,
+                src_ref=sent.at[which, stage], dst_ref=held.at[which, stage, slot],
+                send_sem=gather_send.at[which, stage, d - 1],
+                recv_sem=gather_recv.at[which, stage, slot],
+                device_id=target, device_id_type=MESH,
             ))
         return copies
 
-    def spread(which, axis, value):
-        sent[which * 2 + (0 if axis == "row" else 1)] = value
-        if axis == "row":
-            held_row[which, i] = value
-        else:
-            held_col[which, j] = value
-        for copy in gather_copies(which, axis, False):
+    def spread(which, stage, value):
+        axes, count = stages[stage]
+        me = {"row": i, "col": j, "both": i * C + j}[axes]
+        sent[which, stage] = value
+        held[which, stage, me] = value
+        for copy in gather_copies(which, stage, False):
             copy.start()
 
-    def collect(which, axis):
-        for copy in gather_copies(which, axis, True):
+    def collect(which, stage):
+        for copy in gather_copies(which, stage, True):
             copy.wait_recv()
-        held, count = (held_row, R) if axis == "row" else (held_col, C)
-        total = held[which, 0]
-        for at in range(1, count):
-            total = total + held[which, at]
-        return total
+        terms = [held[which, stage, at] for at in range(stages[stage][1])]
+        while len(terms) > 1:
+            terms = [sum(terms[k + 1 : k + 2], terms[k]) for k in range(0, len(terms), 2)]
+        return terms[0]
 
     sub = lax.broadcasted_iota(jnp.int32, (SUB, LANES), 0)
 
@@ -332,15 +333,15 @@
                 blocks[home] = jnp.where(sub == base + q, done, blocks[home])
         return jnp.concatenate(blocks, axis=0)
 
-    spread(0, "row", gram(lambda r: y1[r + 1, :, 0:cols]))
+    spread(0, 0, gram(lambda r: y1[r + 1, :, 0:cols]))
     rotate(y1, y1_l, y1_r, 0, rows + 2)
     apply((y1_l, y1, y1_r), y2, 1, rows + 1, 1, -1, tiles)
-    second = gram(lambda r: y2[r])
-    spread(1, "row", second)
-    spread(0, "col", collect(0, "row"))
-    spread(1, "col", collect(1, "row"))
-    table_1 = eliminate(collect(0, "col"))
-    table_2 = eliminate(collect(1, "col"))
+    spread(1, 0, gram(lambda r: y2[r]))
+    for stage in range(1, len(stages)):
+        spread(0, stage, collect(0, stage - 1))
+        spread(1, stage, collect(1, stage - 1))
+    table_1 = eliminate(collect(0, len(stages) - 1))
+    table_2 = eliminate(collect(1, len(stages) - 1))
 
     inverse_1 = table_1[:, n : 2 * n]
     upper_2 = table_2[:, 0:n]
@@ -389,18 +390,20 @@
         row_copy(False).wait_send()
 
     for which in range(2):
-        for axis in ("row", "col"):
-            for copy in gather_copies(which, axis, False):
+        for stage in range(len(stages)):
+            for copy in gather_copies(which, stage, False):
                 copy.wait_send()
 
 
 def on_device(sketch, weights):
     n, rows, cols = sketch.shape
     R, C = lax.axis_size("row"), lax.axis_size("col")
+    stages = (("both", R * C),) if R * C <= 16 else (("row", R), ("col", C))
+    peers = max(count for _, count in stages)
     dma = pltpu.SemaphoreType.DMA
     f32 = jnp.float32
     basis, factor = pl.pallas_call(
-        functools.partial(kernel, n, rows, cols, R, C),
+        functools.partial(kernel, n, rows, cols, R, C, stages),
         out_shape=(
             jax.ShapeDtypeStruct((n * rows, cols), f32),
             jax.ShapeDtypeStruct((n, n), f32),
@@ -423,11 +426,10 @@
             pltpu.VMEM((rows, n, cols), f32),
             pltpu.VMEM((2 * SUB, LANES), f32),
             pltpu.VMEM((6, 2 * SUB, LANES), f32),
-            pltpu.VMEM((2, R, SUB, LANES), f32),
-            pltpu.VMEM((2, C, SUB, LANES), f32),
-            pltpu.VMEM((4, SUB, LANES), f32),
+            pltpu.VMEM((2, len(stages), peers, SUB, LANES), f32),
+            pltpu.VMEM((2, len(stages), SUB, LANES), f32),
             dma((2, cols // LANES)), dma((cols // LANES,)), dma((2,)), dma((2,)), dma((6,)), dma((6,)),
-            dma((2, R)), dma((2, R)), dma((2, C)), dma((2, C)),
+            dma((2, len(stages), peers)), dma((2, len(stages), peers)),
         ],
         compiler_params=pltpu.CompilerParams(
             collective_id=0, has_side_effects=True, vmem_limit_bytes=32 * 1024 * 1024

time: 25.1 us -> 23.9 us (0.952)
  Pallas kernels: 20.9 us -> 19.7 us
    pallas_call x1, Pallas kernels: 20.9 us -> 19.7 us  [on_device(): pl.pallas_call(functools.partial(kernel, n, rows, cols, R, C, stages), ou...]
where the time goes in v3:
time: 23.9 us; the launch traced here: 23.7 us
  Pallas kernels  19.7 us (82%)
  local copies, waits for them, and re-layouts  3.34 us (14%)
  between operations  0.65 us (3%)
    pallas_call x1, Pallas kernels, on_device(): pl.pallas_call(functools.partial(kernel, n, rows, cols, R, C, stages), ou...  19.7 us
    unnamed x6, local copies, waits for them, and re-layouts  3.34 us

profile of v3, /device:TPU:0, one launch (start us, length us, event | category | flops | bytes accessed | tf_op | source)
XLA Modules:
  0.0 23.7 jit_solution(1682735988535031663)
XLA Ops:
  0.6 0.0 copy-start
  0.6 1.0 %copy-done = f32[32,8,512]{2,1,0:T(8,128)S(1)} copy-done((f32[32,8,512]{2,1,0:T(8,128)S(1)}, f32[32,8,512]{2,1,0:T(8,128)}, u32[]{:S(2)}) %copy-start) | copy-done | bytes 524312
  1.7 0.0 copy-start.1
  1.7 0.9 %copy-done.1 = f32[8,8,512]{2,1,0:T(8,128)S(1)} copy-done((f32[8,8,512]{2,1,0:T(8,128)S(1)}, f32[8,8,512]{2,1,0:T(8,128)}, u32[]{:S(2)}) %copy-start.1) | copy-done | bytes 131096
  2.6 19.7 %shard_map.41 = (f32[256,512]{1,0:T(8,128)S(1)}, f32[32,32]{1,0:T(8,128)S(1)}) custom-call(f32[256,512]{1,0:T(8,128)S(1)} %bitcast.3, f32[64,512]{1,0:T(8,128)S(1)} %bitcast.5), custom_call_target="tpu_custom_call" | custom-call | tf_op jit(solution)/shard_map/pallas_call | solution.py:405
  22.3 0.8 %copy.6 = f32[32,8,512]{2,1,0:T(8,128)} copy(f32[32,8,512]{2,1,0:T(8,128)S(1)} %bitcast.4) | data formatting | bytes 1048576
  23.1 0.6 %copy.7 = f32[32,32]{1,0:T(8,128)} copy(f32[32,32]{1,0:T(8,128)S(1)} %get-tuple-element.9) | data formatting | bytes 8192
Async XLA Ops:
  0.6 1.0 %copy-start = (f32[32,8,512]{2,1,0:T(8,128)S(1)}, f32[32,8,512]{2,1,0:T(8,128)}, u32[]{:S(2)}) copy-start(f32[32,8,512]{2,1,0:T(8,128)} %param.2) | copy-start | bytes 1572868
  1.7 0.9 %copy-start.1 = (f32[8,8,512]{2,1,0:T(8,128)S(1)}, f32[8,8,512]{2,1,0:T(8,128)}, u32[]{:S(2)}) copy-start(f32[8,8,512]{2,1,0:T(8,128)} %param.3) | copy-start | bytes 393220

commit v4 on v3

--- a/solution.py
+++ b/solution.py
@@ -23,9 +23,9 @@
 
 def kernel(
     n, rows, cols, R, C, stages,
-    sk_hbm, w_hbm, out_ref, fac_ref,
-    raw, wraw, staged, ext, ext_l, ext_r, y1, y1_l, y1_r, y2, pack, nb, held, sent,
-    load_sem, store_sem, row_send, row_recv, nb_send, nb_recv, gather_send, gather_recv,
+    sk_hbm, w_hbm, y2, tables,
+    raw, wraw, ext, ext_l, ext_r, y1, y1_l, y1_r, pack, nb, held, sent,
+    load_sem, row_send, row_recv, nb_send, nb_recv, gather_send, gather_recv,
 ):
     groups = n // SUB
     all_groups = groups + 1
@@ -343,9 +343,35 @@
     table_1 = eliminate(collect(0, len(stages) - 1))
     table_2 = eliminate(collect(1, len(stages) - 1))
 
-    inverse_1 = table_1[:, n : 2 * n]
-    upper_2 = table_2[:, 0:n]
-    inverse_2 = table_2[:, n : 2 * n]
+    tables[0] = table_1
+    tables[1] = table_2
+
+    for dr, ok_r in ups:
+        for dc, ok_c in sides:
+            @pl.when(cond(ok_r, ok_c))
+            def _(dr=dr, dc=dc):
+                edge_copy(dr, dc).wait_send()
+
+    @pl.when(has_down)
+    def _():
+        row_copy(True).wait_send()
+
+    @pl.when(has_up)
+    def _():
+        row_copy(False).wait_send()
+
+    for which in range(2):
+        for stage in range(len(stages)):
+            for copy in gather_copies(which, stage, False):
+                copy.wait_send()
+
+
+def finish(n, rows, cols, y2, tables, out_ref, fac_ref, staged, store_sem):
+    groups = n // SUB
+    tiles = cols // LANES
+    inverse_1 = tables[0, :, n : 2 * n]
+    upper_2 = tables[1, :, 0:n]
+    inverse_2 = tables[1, :, n : 2 * n]
     row_at = lax.broadcasted_iota(jnp.int32, (n, n), 0)
     col_at = lax.broadcasted_iota(jnp.int32, (n, n), 1)
     upper_2 = jnp.where(col_at >= row_at, upper_2, 0.0)
@@ -375,25 +401,6 @@
     for store in stores:
         store.wait()
 
-    for dr, ok_r in ups:
-        for dc, ok_c in sides:
-            @pl.when(cond(ok_r, ok_c))
-            def _(dr=dr, dc=dc):
-                edge_copy(dr, dc).wait_send()
-
-    @pl.when(has_down)
-    def _():
-        row_copy(True).wait_send()
-
-    @pl.when(has_up)
-    def _():
-        row_copy(False).wait_send()
-
-    for which in range(2):
-        for stage in range(len(stages)):
-            for copy in gather_copies(which, stage, False):
-                copy.wait_send()
-
 
 def on_device(sketch, weights):
     n, rows, cols = sketch.shape
@@ -402,39 +409,54 @@
     peers = max(count for _, count in stages)
     dma = pltpu.SemaphoreType.DMA
     f32 = jnp.float32
+    image, tables = pl.pallas_call(
+        functools.partial(kernel, n, rows, cols, R, C, stages),
+        out_shape=(
+            jax.ShapeDtypeStruct((rows, n, cols), f32),
+            jax.ShapeDtypeStruct((2, n, LANES), f32),
+        ),
+        in_specs=[pl.BlockSpec(memory_space=pltpu.HBM)] * 2,
+        out_specs=(
+            pl.BlockSpec(memory_space=pltpu.VMEM),
+            pl.BlockSpec(memory_space=pltpu.VMEM),
+        ),
+        scratch_shapes=[
+            pltpu.VMEM((cols // LANES, n * rows, LANES), f32),
+            pltpu.VMEM((cols // LANES, SUB * rows, LANES), f32),
+            pltpu.VMEM((rows + 4, n + SUB, cols + LANES), f32),
+            pltpu.VMEM((rows + 4, n, cols + LANES), f32),
+            pltpu.VMEM((rows + 4, n, cols + LANES), f32),
+            pltpu.VMEM((rows + 2, n, cols + LANES), f32),
+            pltpu.VMEM((rows + 2, n, cols), f32),
+            pltpu.VMEM((rows + 2, n, cols), f32),
+            pltpu.VMEM((2 * SUB, LANES), f32),
+            pltpu.VMEM((6, 2 * SUB, LANES), f32),
+            pltpu.VMEM((2, len(stages), peers, SUB, LANES), f32),
+            pltpu.VMEM((2, len(stages), SUB, LANES), f32),
+            dma((2, cols // LANES)), dma((2,)), dma((2,)), dma((6,)), dma((6,)),
+            dma((2, len(stages), peers)), dma((2, len(stages), peers)),
+        ],
+        compiler_params=pltpu.CompilerParams(
+            collective_id=0, has_side_effects=True, vmem_limit_bytes=62 * 1024 * 1024
+        ),
+    )(sketch.reshape(n * rows, cols), weights.reshape(SUB * rows, cols))
     basis, factor = pl.pallas_call(
-        functools.partial(kernel, n, rows, cols, R, C, stages),
+        functools.partial(finish, n, rows, cols),
         out_shape=(
             jax.ShapeDtypeStruct((n * rows, cols), f32),
             jax.ShapeDtypeStruct((n, n), f32),
         ),
-        in_specs=[pl.BlockSpec(memory_space=pltpu.HBM)] * 2,
+        in_specs=[pl.BlockSpec(memory_space=pltpu.VMEM)] * 2,
         out_specs=(
             pl.BlockSpec(memory_space=pl.ANY),
             pl.BlockSpec(memory_space=pltpu.VMEM),
         ),
         scratch_shapes=[
             pltpu.VMEM((cols // LANES, n * rows, LANES), f32),
-            pltpu.VMEM((cols // LANES, SUB * rows, LANES), f32),
-            pltpu.VMEM((cols // LANES, n * rows, LANES), f32),
-            pltpu.VMEM((rows + 4, n + SUB, cols + LANES), f32),
-            pltpu.VMEM((rows + 4, n, cols + LANES), f32),
-            pltpu.VMEM((rows + 4, n, cols + LANES), f32),
-            pltpu.VMEM((rows + 2, n, cols + LANES), f32),
-            pltpu.VMEM((rows + 2, n, cols), f32),
-            pltpu.VMEM((rows + 2, n, cols), f32),
-            pltpu.VMEM((rows, n, cols), f32),
-            pltpu.VMEM((2 * SUB, LANES), f32),
-            pltpu.VMEM((6, 2 * SUB, LANES), f32),
-            pltpu.VMEM((2, len(stages), peers, SUB, LANES), f32),
-            pltpu.VMEM((2, len(stages), SUB, LANES), f32),
-            dma((2, cols // LANES)), dma((cols // LANES,)), dma((2,)), dma((2,)), dma((6,)), dma((6,)),
-            dma((2, len(stages), peers)), dma((2, len(stages), peers)),
+            dma((cols // LANES,)),
         ],
-        compiler_params=pltpu.CompilerParams(
-            collective_id=0, has_side_effects=True, vmem_limit_bytes=32 * 1024 * 1024
-        ),
-    )(sketch.reshape(n * rows, cols), weights.reshape(SUB * rows, cols))
+        compiler_params=pltpu.CompilerParams(vmem_limit_bytes=62 * 1024 * 1024),
+    )(image, tables)
     return basis.reshape(n, rows, cols), factor
 
 

time: 23.9 us -> 23.4 us (0.979)
  local copies, waits for them, and re-layouts: 3.34 us -> 0 us
  Pallas kernels: 19.7 us -> 22.6 us
    unnamed x6 -> x0, local copies, waits for them, and re-layouts: 3.34 us -> none
    pallas_call x0 -> x1, Pallas kernels: none -> 2.74 us  [on_device(): pl.pallas_call(functools.partial(finish, n, rows, cols), out_shape=(jax.S...]
where the time goes in v4:
time: 23.4 us; the launch traced here: 23.3 us
  Pallas kernels  22.6 us (97%)
  between operations  0.64 us (3%)
    pallas_call x1, Pallas kernels, on_device(): pl.pallas_call(functools.partial(kernel, n, rows, cols, R, C, stages), ou...  19.9 us
    pallas_call x1, Pallas kernels, on_device(): pl.pallas_call(functools.partial(finish, n, rows, cols), out_shape=(jax.S...  2.74 us

profile of v4, /device:TPU:0, one launch (start us, length us, event | category | flops | bytes accessed | tf_op | source)
XLA Modules:
  0.0 23.3 jit_solution(1405212625821541785)
XLA Ops:
  0.6 19.9 %shard_map.41 = (f32[8,32,512]{2,1,0:T(8,128)}, f32[2,32,128]{2,1,0:T(8,128)}) custom-call(f32[256,512]{1,0:T(8,128)} %bitcast.3, f32[64,512]{1,0:T(8,128)} %bitcast.4), custom_call_target="tpu_custom_call" | custom-call | tf_op jit(solution)/shard_map/pallas_call | solution.py:412
  20.5 2.7 %shard_map.42 = (f32[256,512]{1,0:T(8,128)}, f32[32,32]{1,0:T(8,128)}) custom-call(f32[8,32,512]{2,1,0:T(8,128)} %get-tuple-element.6.y2, f32[2,32,128]{2,1,0:T(8,128)} %get-tuple-element.7.tables), custom_call_target="tpu_custom_call" | custom-call | tf_op jit(solution)/shard_map/pallas_call | solution.py:443
